TPU v7x, 128 devices: a whole 4x4x4 slice. The times are simulated.
128 devices in a mesh: band: 4 (over y), strip: 32 (over x, z, core).
Axes of the slice: x: 4, y: 4, z: 4, core: 2. Of those that a mesh axis runs over, the one named last changes fastest.
Arguments:
- cloud_field: bfloat16 [256, 1024, 512], P('band', 'strip'), may hold values from -6 to 6
- row_gain: float32 [512], replicated, may hold values from 0.1 to 1.9
- row_qkv: bfloat16 [512, 1536], replicated, may hold values from -0.25 to 0.25
- row_out: bfloat16 [512, 512], replicated, may hold values from -1 to 1
- col_gain: float32 [512], replicated, may hold values from 0.1 to 1.9
- col_qkv: bfloat16 [512, 1536], replicated, may hold values from -0.25 to 0.25
- col_out: bfloat16 [512, 512], replicated, may hold values from -1 to 1
- plant_cell: int32 [16384], P(('band', 'strip')), may hold values from 0 to 2047
- plant_decoder_device: int32 [16384, 1], P(('band', 'strip')), may hold values from 0 to 127; in each aligned block of 128 rows (0 to 127, 128 to 255, ...) at most 2 rows name the same one
- plant_capacity: int32 [16384], P(('band', 'strip')), may hold values from 100 to 5000
- decode_first: bfloat16 [65536, 512], P(('band', 'strip')), may hold values from -0.25 to 0.25
- decode_second: bfloat16 [128, 512], P(('band', 'strip')), may hold values from -0.25 to 0.25
Outputs:
- final_field: bfloat16 [256, 1024, 512], P('band', 'strip')
- plant_power: float32 [16384], P(('band', 'strip'))
- fleet_yield: float32 [], replicated
Inputs may be any that keep to these rules, and one draw needn't show every extreme that they name: `plant_decoder_device`: among the 128 plants listed on one device, no owner is named more than 2 times.
All inputs are finite; a program needn't handle non-finite values.
Results may differ from a plain program's by a relative error of at most 0.015.
Values may be sent and summed in bfloat16 or wider, within the bound.
No kernel may reach another device: no remote copies, remote signals or barrier semaphores. Data moves between devices by JAX's collectives and lax.ppermute only.
A program may use at most 64 MiB of HBM per device.

v0:
```python
import math

import jax
import jax.numpy as jnp
from jax import lax
from jax.experimental import pallas as pl
from jax.experimental.pallas import tpu as pltpu
from jax.sharding import PartitionSpec as P

HEADS = 8
EPS = 1e-06
TAU = 12.0
BF = jnp.bfloat16
F32 = jnp.float32
LOG2E = math.log2(math.e)
VMEM_LIMIT = 56 * 1024 * 1024


def _dot(a, b):
    return jnp.dot(a, b, preferred_element_type=F32)


def _dot_t(a, b):
    return lax.dot_general(a, b, (((1,), (1,)), ((), ())), preferred_element_type=F32)


def _norm(x, gain):
    return x * lax.rsqrt(jnp.mean(x * x, axis=-1, keepdims=True) + EPS) * gain


def _get(ref, rows):
    return jnp.concatenate([ref[j, rows, :] for j in range(4)], axis=1)


def _put(ref, rows, value):
    for j in range(4):
        ref[j, rows, :] = value[:, 128 * j : 128 * (j + 1)]


def _first_half(shape):
    return lax.broadcasted_iota(jnp.int32, shape, 1) % 128 < 64


def _project(normed, wqkv_ref, seg_ref, rows, q_s, k0_s, k1_s, v0_s, v1_s):
    half = 256
    seg = seg_ref[...]
    even = _first_half((normed.shape[0], half))
    zero = jnp.zeros((normed.shape[0], half), BF)
    one = jnp.ones((normed.shape[0], half), BF)
    for h in range(2):
        lanes = slice(h * half, (h + 1) * half)
        q = _dot(normed, wqkv_ref[:, h * half : (h + 1) * half])
        scale = lax.rsqrt(_dot((q * q).astype(BF), seg) + EPS)
        q_s[rows, lanes] = (q * (scale * (TAU / 64 * LOG2E))).astype(BF)
        k = _dot(normed, wqkv_ref[:, 512 + h * half : 512 + (h + 1) * half])
        scale = lax.rsqrt(_dot((k * k).astype(BF), seg) + EPS)
        k = (k * scale).astype(BF)
        k0_s[rows, lanes] = jnp.where(even, k, zero)
        k1_s[rows, lanes] = jnp.where(even, zero, k)
        v = _dot(normed, wqkv_ref[:, 1024 + h * half : 1024 + (h + 1) * half]).astype(BF)
        v0_s[rows, lanes] = jnp.where(even, v, one)
        v1_s[rows, lanes] = jnp.where(even, one, v)


def _pair(q, k0, k1, v0, v1):
    o0 = _dot(jnp.exp2(_dot_t(q, k0)).astype(BF), v0)
    o1 = _dot(jnp.exp2(_dot_t(q, k1)).astype(BF), v1)
    even = _first_half(o0.shape)
    total = pltpu.roll(jnp.where(even, o1, o0), 64, 1)
    return (jnp.where(even, o0, o1) / total).astype(BF)


def _row_kernel(x_ref, g_ref, wqkv_ref, wo_ref, seg_ref, out_ref, q_s, k0_s, k1_s, v0_s, v1_s, c_s):
    tok, blk = 1024, 256
    gain = g_ref[...]
    for t in range(tok // blk):
        x = x_ref[8 * t : 8 * t + 8, 0].reshape(blk, 512).astype(F32)
        _project(
            _norm(x, gain).astype(BF), wqkv_ref, seg_ref, slice(t * blk, (t + 1) * blk), q_s, k0_s, k1_s, v0_s, v1_s
        )

    def step(i, _):
        lanes = pl.ds(pl.multiple_of(i * 128, 128), 128)
        k0, k1, v0, v1 = k0_s[:, lanes], k1_s[:, lanes], v0_s[:, lanes], v1_s[:, lanes]
        for t in range(tok // blk):
            rows = slice(t * blk, (t + 1) * blk)
            c_s[rows, lanes] = _pair(q_s[rows, lanes], k0, k1, v0, v1)
        return 0

    lax.fori_loop(0, 4, step, 0)
    for t in range(tok // blk):
        x = x_ref[8 * t : 8 * t + 8, 0].reshape(blk, 512).astype(F32)
        y = (x + _dot(c_s[t * blk : (t + 1) * blk, :], wo_ref[...])).astype(BF).reshape(8, 4, 8, 512)
        for b in range(4):
            out_ref[b, 8 * t : 8 * t + 8] = y[:, b]


def row_layer(x, which, gain, wqkv, wo, seg):
    tokens = pltpu.VMEM((1024, 512), BF)
    whole = lambda *shape: pl.BlockSpec(shape, lambda i: (0,) * len(shape))
    return pl.pallas_call(
        _row_kernel,
        grid=(1,),
        out_shape=jax.ShapeDtypeStruct((4, 32, 8, 512), BF),
        in_specs=[
            pl.BlockSpec((32, 1, 32, 512), lambda i: (0, which, 0, 0)),
            whole(1, 512),
            whole(512, 1536),
            whole(512, 512),
            whole(256, 256),
        ],
        out_specs=whole(4, 32, 8, 512),
        scratch_shapes=[tokens] * 6,
        compiler_params=pltpu.CompilerParams(vmem_limit_bytes=VMEM_LIMIT),
        cost_estimate=pl.CostEstimate(flops=12_000_000_000, bytes_accessed=4_000_000, transcendentals=8_000_000),
        name="row_layer",
    )(x, gain, wqkv, wo, seg)


def _col_kernel(
    x0_ref, x1_ref, g_ref, wqkv_ref, wo_ref, seg_ref, idx_ref, y_ref, send_ref,
    wide_s, q_s, k0_s, k1_s, v0_s, v1_s, c_s,
):
    blk = 256
    gain = g_ref[...]
    for r, x_ref in enumerate((x0_ref, x1_ref)):
        for t in range(4):
            x = x_ref[32 * t : 32 * t + 32].reshape(blk, 512).astype(F32)
            _put(wide_s, slice(r * 1024 + t * blk, r * 1024 + (t + 1) * blk), _norm(x, gain))

    def project(c, _):
        normed = _get(wide_s, pl.ds(c, 256, stride=8)).astype(BF)
        rows = pl.ds(pl.multiple_of(c * 256, 256), 256)
        _project(normed, wqkv_ref, seg_ref, rows, q_s, k0_s, k1_s, v0_s, v1_s)
        return 0

    lax.fori_loop(0, 8, project, 0)

    def attend(c, _):
        rows = pl.ds(pl.multiple_of(c * 256, 256), 256)
        for p in range(4):
            lanes = slice(p * 128, (p + 1) * 128)
            c_s[rows, lanes] = _pair(
                q_s[rows, lanes], k0_s[rows, lanes], k1_s[rows, lanes], v0_s[rows, lanes], v1_s[rows, lanes]
            )
        _put(wide_s, pl.ds(c, 256, stride=8), _dot(c_s[rows, :], wo_ref[...]))
        return 0

    lax.fori_loop(0, 8, attend, 0)
    for r, x_ref in enumerate((x0_ref, x1_ref)):
        for t in range(4):
            x = x_ref[32 * t : 32 * t + 32].reshape(blk, 512).astype(F32)
            y = x + _get(wide_s, slice(r * 1024 + t * blk, r * 1024 + (t + 1) * blk))
            y_ref[32 * t : 32 * t + 32, r] = y.astype(BF).reshape(32, 8, 512)
    for b in range(4):
        y = y_ref[32 * b : 32 * b + 32].reshape(512, 512)
        for m in range(2):
            k = 2 * b + m
            pick = lax.broadcasted_iota(jnp.int32, (128, 512), 1) == idx_ref[:, k : k + 1]
            _put(wide_s, pl.ds(k, 128, stride=8), _dot(pick.astype(F32).astype(BF), y))
    send_ref[...] = _get(wide_s, slice(0, 1024)).astype(BF).reshape(128, 8, 512)


def col_layer(x0, x1, gain, wqkv, wo, seg, idx):
    tokens = pltpu.VMEM((2048, 512), BF)
    return pl.pallas_call(
        _col_kernel,
        out_shape=(jax.ShapeDtypeStruct((128, 2, 8, 512), BF), jax.ShapeDtypeStruct((128, 8, 512), BF)),
        in_specs=[pl.BlockSpec(memory_space=pltpu.VMEM)] * 7,
        out_specs=(pl.BlockSpec(memory_space=pltpu.VMEM),) * 2,
        scratch_shapes=[pltpu.VMEM((4, 2048, 128), F32)] + [tokens] * 6,
        compiler_params=pltpu.CompilerParams(vmem_limit_bytes=VMEM_LIMIT),
        cost_estimate=pl.CostEstimate(flops=12_000_000_000, bytes_accessed=9_000_000, transcendentals=4_000_000),
        name="col_layer",
    )(x0, x1, gain, wqkv, wo, seg, idx)


def _decode_kernel(f_ref, w1_ref, w2_ref, cap_ref, out_ref, logit_s):
    w2 = jnp.broadcast_to(w2_ref[...], (128, 512))
    for t in range(4):
        feats = f_ref[32 * t : 32 * t + 32].reshape(256, 512)
        hidden = jax.nn.gelu(_dot(feats, w1_ref[...])).astype(BF)
        logit_s[t * 256 : (t + 1) * 256, :] = _dot_t(hidden, w2)
    lane = lax.broadcasted_iota(jnp.int32, (32, 128), 1)
    power = jnp.zeros((32, 128), F32)
    sums = []
    for k in range(8):
        logit = logit_s[pl.ds(k, 128, stride=8), :]
        cap = cap_ref[:, k : k + 1]
        value = jnp.maximum(logit, 0.0) + jnp.log1p(jnp.exp(-jnp.abs(logit)))
        value = jnp.where(cap > 0, value, 0.0)
        weighted = value * (cap * 0.001)
        fold = lambda a: (a[0:32] + a[32:64]) + (a[64:96] + a[96:128])
        sums.append(fold(value))
        power = power + fold(weighted)
    total = jnp.sum(power, axis=0, keepdims=True)
    for b in range(4):
        rows = jnp.where(lane == 0, sums[2 * b], jnp.where(lane == 1, sums[2 * b + 1], total))
        out_ref[32 * b : 32 * b + 32, :] = rows


def decode(features, w1, w2, caps):
    return pl.pallas_call(
        _decode_kernel,
        out_shape=jax.ShapeDtypeStruct((128, 128), F32),
        scratch_shapes=[pltpu.VMEM((1024, 128), F32)],
        compiler_params=pltpu.CompilerParams(vmem_limit_bytes=VMEM_LIMIT),
        cost_estimate=pl.CostEstimate(flops=600_000_000, bytes_accessed=2_000_000, transcendentals=600_000),
        name="decode",
    )(features, w1, w2, caps)


def _power_kernel(back_ref, owner_ref, slot_ref, cap_ref, power_ref, fleet_ref):
    back = back_ref[...]
    named = lax.broadcasted_iota(jnp.int32, (128, 128), 0) == owner_ref[...]
    first = jnp.sum(jnp.where(named, back[:, 0:1], 0.0), axis=0, keepdims=True)
    second = jnp.sum(jnp.where(named, back[:, 1:2], 0.0), axis=0, keepdims=True)
    value = jnp.where(slot_ref[...] == 0, first, second)
    power_ref[...] = cap_ref[...].astype(F32) * 0.001 * value
    fleet_ref[...] = jnp.sum(back, axis=0, keepdims=True) / 16384.0


def power(back, owner, slot, cap):
    return pl.pallas_call(
        _power_kernel,
        out_shape=(jax.ShapeDtypeStruct((1, 128), F32), jax.ShapeDtypeStruct((1, 128), F32)),
        name="plant_power",
    )(back, owner, slot, cap)


def body(
    cloud_field, row_gain, row_qkv, row_out, col_gain, col_qkv, col_out,
    plant_cell, plant_decoder_device, plant_capacity, decode_first, decode_second,
):
    everyone = ("band", "strip")
    a2a = lambda x, axis: lax.all_to_all(x, axis, split_axis=0, concat_axis=0, tiled=True)
    seg_of = jnp.arange(256) // 64
    seg = jnp.where(seg_of[:, None] == seg_of[None, :], 1.0 / 64, 0.0).astype(BF)
    tokens = a2a(cloud_field.reshape(32, 2, 32, 512), "strip")

    owner = plant_decoder_device[:, 0]
    listed = lax.all_gather(jnp.stack([plant_cell, owner, plant_capacity]), "band")
    cell_all, owner_all, cap_all = listed[:, 0], listed[:, 1], listed[:, 2]
    earlier = jnp.arange(128)[None, :] < jnp.arange(128)[:, None]
    same = (owner_all[:, :, None] == owner_all[:, None, :]) & earlier[None]
    slot_all = jnp.sum(same.astype(jnp.int32), axis=2)
    mine = (cell_all % 32) // 8 == lax.axis_index("band")
    token = jnp.where(mine, (cell_all // 32) * 8 + cell_all % 8, -1)
    there = (owner_all[:, None, :] == jnp.arange(128)[None, :, None])[:, :, None, :] & (
        slot_all[:, None, None, :] == jnp.arange(2)[None, None, :, None]
    )
    there = there & mine[:, None, None, :]
    idx = jnp.sum(jnp.where(there, token[:, None, None, :] + 1, 0), axis=-1) - 1
    caps = jnp.sum(jnp.where(there, cap_all[:, None, None, :], 0), axis=-1).astype(F32)
    idx = idx.transpose(1, 0, 2).reshape(128, 8)
    caps = caps.transpose(1, 0, 2).reshape(128, 8)
    caps = jnp.pad(caps, ((0, 0), (0, 120))).reshape(128, 1, 128)
    caps = a2a(caps, everyone).reshape(128, 128)
    my_same = (owner[:, None] == owner[None, :]) & earlier.T
    my_slot = jnp.sum(my_same.astype(jnp.int32), axis=0)

    row_args = (row_gain.reshape(1, 512), row_qkv, row_out, seg)
    sent0 = a2a(row_layer(tokens, 0, *row_args).reshape(128, 8, 512), everyone)
    sent1 = a2a(row_layer(tokens, 1, *row_args).reshape(128, 8, 512), everyone)
    columns, features = col_layer(sent0, sent1, col_gain.reshape(1, 512), col_qkv, col_out, seg, idx)
    features = a2a(features, everyone)
    field = a2a(columns.reshape(4, 64, 8, 512), "band")
    final_field = field.transpose(1, 0, 2, 3).reshape(64, 32, 512)
    payload = decode(features, decode_first, decode_second, caps)
    back = a2a(payload.reshape(128, 1, 128), everyone).reshape(128, 128)
    plant_power, fleet = power(
        back, owner.reshape(1, 128), my_slot.reshape(1, 128), plant_capacity.reshape(1, 128)
    )
    return (final_field, plant_power.reshape(128), fleet[0, 2])


def solution(mesh):
    return jax.shard_map(
        body,
        mesh=mesh,
        in_specs=(
            P("band", "strip", None),
            P(),
            P(),
            P(),
            P(),
            P(),
            P(),
            P(("band", "strip")),
            P(("band", "strip"), None),
            P(("band", "strip")),
            P(("band", "strip"), None),
            P(("band", "strip"), None),
        ),
        out_specs=(P("band", "strip", None), P(("band", "strip")), P()),
        check_vma=False,
    )
```

profile of v0, /device:TPU:1, one launch (start us, length us, event | category | flops | bytes accessed | tf_op | source)
XLA Modules:
  0.0 214.1 jit_solution(12886179449301635265)
XLA Ops:
  0.6 0.0 copy-start.4
  0.6 0.0 copy-start.5
  0.7 0.0 copy-start.6
  0.7 9.6 %all-to-all-start = ((bf16[32,2,32,512]{3,2,1,0:T(8,128)(2,1)}), bf16[32,2,32,512]{3,2,1,0:T(8,128)(2,1)S(1)}, u32[]{:S(2)}, u32[]{:S(2)}) async-start(bf16[32,2,32,512]{3,2,1,0:T(8,128)(2,1)} %bitcast.36), calls=%async_computation | async-start | bytes 4194304 | tf_op jit(solution)/shard_map/all_to_all | solution.py:236
  10.2 0.0 copy-done.4
  10.3 0.0 copy-done.5
  10.3 0.0 copy-done.6
  10.3 9.1 %all-gather.1 = s32[4,3,128]{2,1,0:T(4,128)S(1)} all-gather(s32[1,3,128]{2,1,0:T(4,128)S(1)} %add_bitcast_fusion), channel_id=2, replica_groups=mesh['band'=4,'strip'=32] {'band'}, dimensions={0}, use_global_device_ids=true | all-gather | bytes 7680 | tf_op jit(solution)/shard_map/all_gather | solution.py:242
  19.4 0.2 convert_reduce_fusion
  19.7 0.8 select_convert_fusion.seg_ref
  20.4 18.1 %all-to-all-done.x_ref = bf16[32,2,32,512]{3,2,1,0:T(8,128)(2,1)S(1)} async-done(((bf16[32,2,32,512]{3,2,1,0:T(8,128)(2,1)}), bf16[32,2,32,512]{3,2,1,0:T(8,128)(2,1)S(1)}, u32[]{:S(2)}, u32[]{:S(2)}) %all-to-all-start) | async-done | bytes 2097184 | tf_op jit(solution)/shard_map/all_to_all | solution.py:236
  38.5 0.0 copy-start
  38.5 1.3 copy-done
  39.9 16.2 %row_layer.2 = bf16[4,32,8,512]{3,2,1,0:T(8,128)(2,1)} custom-call(bf16[32,2,32,512]{3,2,1,0:T(8,128)(2,1)} %copy-done, f32[1,512]{1,0:T(1,128)} %bitcast.56, bf16[512,1536]{1,0:T(8,128)(2,1)} %wqkv_ref.4, bf16[512,512]{1,0:T(8,128)(2,1)} %wo_ref.4, bf16[256,256]{1,0:T(8,128)(2,1)} %select_convert_fusion.seg_ref), custom_call_target="tpu_custom_call" | custom-call | flops 12000000000 | bytes 4000000 | tf_op jit(solution)/shard_map/row_layer/pallas_call | solution.py:101
  56.1 5.9 %all-to-all-start.1 = ((bf16[128,8,512]{2,1,0:T(8,128)(2,1)}), bf16[128,8,512]{2,1,0:T(8,128)(2,1)S(1)}, u32[]{:S(2)}, u32[]{:S(2)}) async-start(bf16[128,8,512]{2,1,0:T(8,128)(2,1)} %bitcast.39), calls=%async_computation.1 | async-start | bytes 2097152 | tf_op jit(solution)/shard_map/all_to_all | solution.py:236
  62.0 16.2 %row_layer.3 = bf16[4,32,8,512]{3,2,1,0:T(8,128)(2,1)} custom-call(bf16[32,2,32,512]{3,2,1,0:T(8,128)(2,1)} %copy-done, f32[1,512]{1,0:T(1,128)} %bitcast.57, bf16[512,1536]{1,0:T(8,128)(2,1)} %wqkv_ref.4, bf16[512,512]{1,0:T(8,128)(2,1)} %wo_ref.4, bf16[256,256]{1,0:T(8,128)(2,1)} %select_convert_fusion.seg_ref), custom_call_target="tpu_custom_call" | custom-call | flops 12000000000 | bytes 4000000 | tf_op jit(solution)/shard_map/row_layer/pallas_call | solution.py:101
  78.3 2.9 %all-to-all-done.1.x0_ref = bf16[128,8,512]{2,1,0:T(8,128)(2,1)S(1)} async-done(((bf16[128,8,512]{2,1,0:T(8,128)(2,1)}), bf16[128,8,512]{2,1,0:T(8,128)(2,1)S(1)}, u32[]{:S(2)}, u32[]{:S(2)}) %all-to-all-start.1) | async-done | bytes 1048608 | tf_op jit(solution)/shard_map/all_to_all | solution.py:236
  81.2 0.0 copy-start.1
  81.2 6.8 %all-to-all-start.2 = ((bf16[128,8,512]{2,1,0:T(8,128)(2,1)}), bf16[128,8,512]{2,1,0:T(8,128)(2,1)S(1)}, u32[]{:S(2)}, u32[]{:S(2)}) async-start(bf16[128,8,512]{2,1,0:T(8,128)(2,1)} %bitcast.38), calls=%async_computation.2 | async-start | bytes 2097152 | tf_op jit(solution)/shard_map/all_to_all | solution.py:236
  88.1 0.4 select_reduce_fusion
  88.5 0.7 copy.23.idx_ref
  89.2 0.7 copy.25
  90.0 17.2 %all-to-all-done.2.x1_ref = bf16[128,8,512]{2,1,0:T(8,128)(2,1)S(1)} async-done(((bf16[128,8,512]{2,1,0:T(8,128)(2,1)}), bf16[128,8,512]{2,1,0:T(8,128)(2,1)S(1)}, u32[]{:S(2)}, u32[]{:S(2)}) %all-to-all-start.2) | async-done | bytes 1048608 | tf_op jit(solution)/shard_map/all_to_all | solution.py:236
  107.2 0.0 copy-start.2
  107.2 4.6 %all-to-all-start.5 = ((f32[128,1,128]{2,1,0:T(1,128)}), f32[128,1,128]{2,1,0:T(1,128)S(1)}, u32[]{:S(2)}, u32[]{:S(2)}) async-start(f32[128,1,128]{2,1,0:T(1,128)} %copy.25), calls=%async_computation.5 | async-start | bytes 131072 | tf_op jit(solution)/shard_map/all_to_all | solution.py:236
  111.8 0.0 copy-done.1
  111.8 0.0 copy-done.2
  111.8 24.0 %col_layer.1 = (bf16[128,2,8,512]{3,2,1,0:T(8,128)(2,1)}, bf16[128,8,512]{2,1,0:T(8,128)(2,1)}) custom-call(bf16[128,8,512]{2,1,0:T(8,128)(2,1)} %copy-done.1, bf16[128,8,512]{2,1,0:T(8,128)(2,1)} %copy-done.2, f32[1,512]{1,0:T(1,128)} %bitcast.58, bf16[512,1536]{1,0:T(8,128)(2,1)} %wqkv_ref.5, bf16[512,512]{1,0:T(8,128)(2,1)} %wo_ref.5, ...), custom_call_target="tpu_custom_call" | custom-call | flops 12000000000 | bytes 9000000 | tf_op jit(solution)/shard_map/col_layer/pallas_call | solution.py:166
  135.8 0.0 all-to-all-done.5
  135.8 0.0 copy-start.3
  135.8 29.2 %all_to_all.35.f_ref = bf16[128,8,512]{2,1,0:T(8,128)(2,1)} all-to-all(bf16[128,8,512]{2,1,0:T(8,128)(2,1)} %get-tuple-element.8), channel_id=1, replica_groups=mesh['band'=4,'strip'=32] {'band','strip'}, dimensions={0} | all-to-all | bytes 2097152 | tf_op jit(solution)/shard_map/all_to_all | solution.py:236
  165.0 0.0 copy-done.3
  165.0 3.6 %decode.1 = f32[128,128]{1,0:T(8,128)} custom-call(bf16[128,8,512]{2,1,0:T(8,128)(2,1)} %all_to_all.35.f_ref, bf16[512,512]{1,0:T(8,128)(2,1)} %w1_ref.1, bf16[1,512]{1,0:T(2,128)(2,1)} %w2_ref.1, f32[128,128]{1,0:T(8,128)} %bitcast.41), custom_call_target="tpu_custom_call" | custom-call | flops 600000000 | bytes 2000000 | tf_op jit(solution)/shard_map/decode/pallas_call | solution.py:203
  168.6 15.2 %all_to_all.36 = f32[128,1,128]{2,1,0:T(1,128)} all-to-all(f32[128,1,128]{2,1,0:T(1,128)} %bitcast.42), channel_id=1, replica_groups=mesh['band'=4,'strip'=32] {'band','strip'}, dimensions={0} | all-to-all | bytes 131072 | tf_op jit(solution)/shard_map/all_to_all | solution.py:236
  183.8 3.6 %all-to-all-start.3 = ((bf16[4,64,8,512]{3,2,1,0:T(8,128)(2,1)}), bf16[4,64,8,512]{3,2,1,0:T(8,128)(2,1)S(1)}, u32[]{:S(2)}, u32[]{:S(2)}) async-start(bf16[4,64,8,512]{3,2,1,0:T(8,128)(2,1)} %bitcast.37), calls=%async_computation.3 | async-start | bytes 4194304 | tf_op jit(solution)/shard_map/all_to_all | solution.py:236
  187.4 0.6 convert_reduce_fusion.1
  188.0 1.5 plant_power.1
  189.5 1.2 slice.15
  190.7 21.8 %all-to-all-done.3 = bf16[4,64,8,512]{3,2,1,0:T(8,128)(2,1)S(1)} async-done(((bf16[4,64,8,512]{3,2,1,0:T(8,128)(2,1)}), bf16[4,64,8,512]{3,2,1,0:T(8,128)(2,1)S(1)}, u32[]{:S(2)}, u32[]{:S(2)}) %all-to-all-start.3) | async-done | bytes 2097184 | tf_op jit(solution)/shard_map/all_to_all | solution.py:236
  212.5 1.6 copy_bitcast_fusion
  (10 shorter events, 0.1 us)
Async XLA Ops:
  0.6 9.6 %copy-start.4 = (s32[128]{0:T(128)S(1)}, s32[128]{0:T(128)}, u32[]{:S(2)}) copy-start(s32[128]{0:T(128)} %param.21) | copy-start | bytes 1540
  0.6 9.6 %copy-start.5 = (s32[128,1]{0,1:T(1,128)S(1)}, s32[128,1]{0,1:T(1,128)}, u32[]{:S(2)}) copy-start(s32[128,1]{0,1:T(1,128)} %param.20) | copy-start | bytes 1540
  0.7 9.6 %copy-start.6 = (s32[128]{0:T(128)S(1)}, s32[128]{0:T(128)}, u32[]{:S(2)}) copy-start(s32[128]{0:T(128)} %param.19) | copy-start | bytes 1540
  0.7 37.9 %all-to-all-start = ((bf16[32,2,32,512]{3,2,1,0:T(8,128)(2,1)}), bf16[32,2,32,512]{3,2,1,0:T(8,128)(2,1)S(1)}, u32[]{:S(2)}, u32[]{:S(2)}) async-start(bf16[32,2,32,512]{3,2,1,0:T(8,128)(2,1)} %bitcast.36), calls=%async_computation | async-start | bytes 4194304 | tf_op jit(solution)/shard_map/all_to_all | solution.py:236
  38.5 1.3 copy-start
  56.1 25.1 %all-to-all-start.1 = ((bf16[128,8,512]{2,1,0:T(8,128)(2,1)}), bf16[128,8,512]{2,1,0:T(8,128)(2,1)S(1)}, u32[]{:S(2)}, u32[]{:S(2)}) async-start(bf16[128,8,512]{2,1,0:T(8,128)(2,1)} %bitcast.39), calls=%async_computation.1 | async-start | bytes 2097152 | tf_op jit(solution)/shard_map/all_to_all | solution.py:236
  81.2 30.6 %copy-start.1 = (bf16[128,8,512]{2,1,0:T(8,128)(2,1)}, bf16[128,8,512]{2,1,0:T(8,128)(2,1)S(1)}, u32[]{:S(2)}) copy-start(bf16[128,8,512]{2,1,0:T(8,128)(2,1)S(1)} %all-to-all-done.1.x0_ref) | copy-start | bytes 3145732
  81.2 26.0 %all-to-all-start.2 = ((bf16[128,8,512]{2,1,0:T(8,128)(2,1)}), bf16[128,8,512]{2,1,0:T(8,128)(2,1)S(1)}, u32[]{:S(2)}, u32[]{:S(2)}) async-start(bf16[128,8,512]{2,1,0:T(8,128)(2,1)} %bitcast.38), calls=%async_computation.2 | async-start | bytes 2097152 | tf_op jit(solution)/shard_map/all_to_all | solution.py:236
  107.2 4.6 %copy-start.2 = (bf16[128,8,512]{2,1,0:T(8,128)(2,1)}, bf16[128,8,512]{2,1,0:T(8,128)(2,1)S(1)}, u32[]{:S(2)}) copy-start(bf16[128,8,512]{2,1,0:T(8,128)(2,1)S(1)} %all-to-all-done.2.x1_ref) | copy-start | bytes 3145732
  107.2 28.7 %all-to-all-start.5 = ((f32[128,1,128]{2,1,0:T(1,128)}), f32[128,1,128]{2,1,0:T(1,128)S(1)}, u32[]{:S(2)}, u32[]{:S(2)}) async-start(f32[128,1,128]{2,1,0:T(1,128)} %copy.25), calls=%async_computation.5 | async-start | bytes 131072 | tf_op jit(solution)/shard_map/all_to_all | solution.py:236
  135.8 29.2 %copy-start.3 = (f32[128,1,128]{2,1,0:T(1,128)}, f32[128,1,128]{2,1,0:T(1,128)S(1)}, u32[]{:S(2)}) copy-start(f32[128,1,128]{2,1,0:T(1,128)S(1)} %all-to-all-done.5) | copy-start | bytes 196612
  183.8 28.7 %all-to-all-start.3 = ((bf16[4,64,8,512]{3,2,1,0:T(8,128)(2,1)}), bf16[4,64,8,512]{3,2,1,0:T(8,128)(2,1)S(1)}, u32[]{:S(2)}, u32[]{:S(2)}) async-start(bf16[4,64,8,512]{3,2,1,0:T(8,128)(2,1)} %bitcast.37), calls=%async_computation.3 | async-start | bytes 4194304 | tf_op jit(solution)/shard_map/all_to_all | solution.py:236
where the time goes:
time: 216 us; the launch traced here: 214 us
  Pallas kernels  61.5 us (28%)
  waiting for transfers between devices  60 us (28%)
  blocking collectives  53.5 us (25%)
  starting transfers between devices  30.5 us (14%)
  local copies, waits for them, and re-layouts  5.67 us (3%)
    all_to_all x5, waiting for transfers between devices, body(): lax.all_to_all(x, axis, split_axis=0, concat_axis=0, tiled=True)  60 us
    all_to_all x2, blocking collectives, body(): lax.all_to_all(x, axis, split_axis=0, concat_axis=0, tiled=True)  44.4 us
    pallas_call x2, Pallas kernels, row_layer(): pl.pallas_call(_row_kernel, grid=(1,), out_shape=jax.ShapeDtypeStruct((4,...  32.5 us
    all_to_all x5, starting transfers between devices, body(): lax.all_to_all(x, axis, split_axis=0, concat_axis=0, tiled=True)  30.5 us
    pallas_call x1, Pallas kernels, col_layer(): pl.pallas_call(_col_kernel, out_shape=(jax.ShapeDtypeStruct((128, 2, 8, 5...  24 us
    all_gather x1, blocking collectives, body(): lax.all_gather(jnp.stack([plant_cell, owner, plant_capacity]), 'band')  9.11 us
  transfers between devices with their start and end apart: 5, of which 4 were waited for; matrix products, arithmetic and copies ran while one was open for 2% of the time, Pallas kernels for 19%

commit v1 on v0

--- a/solution.py
+++ b/solution.py
@@ -87,7 +87,7 @@
             c_s[rows, lanes] = _pair(q_s[rows, lanes], k0, k1, v0, v1)
         return 0
 
-    lax.fori_loop(0, 4, step, 0)
+    lax.fori_loop(0, 4, step, 0, unroll=4)
     for t in range(tok // blk):
         x = x_ref[8 * t : 8 * t + 8, 0].reshape(blk, 512).astype(F32)
         y = (x + _dot(c_s[t * blk : (t + 1) * blk, :], wo_ref[...])).astype(BF).reshape(8, 4, 8, 512)
@@ -117,10 +117,16 @@
     )(x, gain, wqkv, wo, seg)
 
 
+def _rank(named):
+    before = lax.broadcasted_iota(jnp.int32, (128, 128), 0) < lax.broadcasted_iota(jnp.int32, (128, 128), 1)
+    return _dot(named.astype(F32).astype(BF), before.astype(F32).astype(BF)).astype(jnp.int32)
+
+
 def _col_kernel(
-    x0_ref, x1_ref, g_ref, wqkv_ref, wo_ref, seg_ref, idx_ref, y_ref, send_ref,
+    x0_ref, x1_ref, g_ref, wqkv_ref, wo_ref, seg_ref, listed_ref, me_ref, y0_ref, y1_ref, y2_ref, y3_ref, send_ref,
     wide_s, q_s, k0_s, k1_s, v0_s, v1_s, c_s,
 ):
+    band, strip = me_ref[0], me_ref[1]
     blk = 256
     gain = g_ref[...]
     for r, x_ref in enumerate((x0_ref, x1_ref)):
@@ -134,7 +140,7 @@
         _project(normed, wqkv_ref, seg_ref, rows, q_s, k0_s, k1_s, v0_s, v1_s)
         return 0
 
-    lax.fori_loop(0, 8, project, 0)
+    lax.fori_loop(0, 8, project, 0, unroll=8)
 
     def attend(c, _):
         rows = pl.ds(pl.multiple_of(c * 256, 256), 256)
@@ -146,86 +152,136 @@
         _put(wide_s, pl.ds(c, 256, stride=8), _dot(c_s[rows, :], wo_ref[...]))
         return 0
 
-    lax.fori_loop(0, 8, attend, 0)
-    for r, x_ref in enumerate((x0_ref, x1_ref)):
-        for t in range(4):
-            x = x_ref[32 * t : 32 * t + 32].reshape(blk, 512).astype(F32)
-            y = x + _get(wide_s, slice(r * 1024 + t * blk, r * 1024 + (t + 1) * blk))
-            y_ref[32 * t : 32 * t + 32, r] = y.astype(BF).reshape(32, 8, 512)
-    for b in range(4):
-        y = y_ref[32 * b : 32 * b + 32].reshape(512, 512)
+    lax.fori_loop(0, 8, attend, 0, unroll=4)
+    for d, y_ref in enumerate((y0_ref, y1_ref, y2_ref, y3_ref)):
+        to = lax.rem(band + d, 4)
+        for r, x_ref in enumerate((x0_ref, x1_ref)):
+            x = x_ref[pl.ds(32 * to, 32)].reshape(blk, 512).astype(F32)
+            y = x + _get(wide_s, pl.ds(pl.multiple_of(r * 1024 + to * blk, blk), blk))
+            y_ref[:, r] = y.astype(BF).reshape(32, 8, 512)
+    for d, y_ref in enumerate((y0_ref, y1_ref, y2_ref, y3_ref)):
+        lister = lax.rem(band + d, 4) * 32 + strip
+        y = y_ref[...].reshape(512, 512)
+        cell, owner = listed_ref[lister, 0:1, :], listed_ref[lister, 1:2, :]
+        named = lax.broadcasted_iota(jnp.int32, (128, 128), 0) == owner
+        rank = _rank(named)
+        token = jnp.where((cell % 32) // 8 == band, (cell // 32) * 8 + cell % 8 + 1, 0)
         for m in range(2):
-            k = 2 * b + m
-            pick = lax.broadcasted_iota(jnp.int32, (128, 512), 1) == idx_ref[:, k : k + 1]
-            _put(wide_s, pl.ds(k, 128, stride=8), _dot(pick.astype(F32).astype(BF), y))
+            at = jnp.sum(jnp.where(named & (rank == m), token, 0), axis=1, keepdims=True) - 1
+            pick = lax.broadcasted_iota(jnp.int32, (128, 512), 1) == at
+            _put(wide_s, pl.ds(2 * d + m, 128, stride=8), _dot(pick.astype(F32).astype(BF), y))
     send_ref[...] = _get(wide_s, slice(0, 1024)).astype(BF).reshape(128, 8, 512)
 
 
-def col_layer(x0, x1, gain, wqkv, wo, seg, idx):
+VM = pl.BlockSpec(memory_space=pltpu.VMEM)
+SM = pl.BlockSpec(memory_space=pltpu.SMEM)
+ANY = pl.BlockSpec(memory_space=pl.ANY)
+
+
+def col_layer(x0, x1, gain, wqkv, wo, seg, listed, me):
     tokens = pltpu.VMEM((2048, 512), BF)
+    part = jax.ShapeDtypeStruct((32, 2, 8, 512), BF)
     return pl.pallas_call(
         _col_kernel,
-        out_shape=(jax.ShapeDtypeStruct((128, 2, 8, 512), BF), jax.ShapeDtypeStruct((128, 8, 512), BF)),
-        in_specs=[pl.BlockSpec(memory_space=pltpu.VMEM)] * 7,
-        out_specs=(pl.BlockSpec(memory_space=pltpu.VMEM),) * 2,
+        out_shape=(part,) * 4 + (jax.ShapeDtypeStruct((128, 8, 512), BF),),
+        in_specs=[VM] * 7 + [SM],
+        out_specs=(VM,) * 5,
         scratch_shapes=[pltpu.VMEM((4, 2048, 128), F32)] + [tokens] * 6,
         compiler_params=pltpu.CompilerParams(vmem_limit_bytes=VMEM_LIMIT),
         cost_estimate=pl.CostEstimate(flops=12_000_000_000, bytes_accessed=9_000_000, transcendentals=4_000_000),
         name="col_layer",
-    )(x0, x1, gain, wqkv, wo, seg, idx)
-
-
-def _decode_kernel(f_ref, w1_ref, w2_ref, cap_ref, out_ref, logit_s):
+    )(x0, x1, gain, wqkv, wo, seg, listed, me)
+
+
+def _decode_kernel(f_ref, w1_ref, w2_ref, listed_ref, me_ref, out_ref, logit_s):
     w2 = jnp.broadcast_to(w2_ref[...], (128, 512))
     for t in range(4):
         feats = f_ref[32 * t : 32 * t + 32].reshape(256, 512)
         hidden = jax.nn.gelu(_dot(feats, w1_ref[...])).astype(BF)
         logit_s[t * 256 : (t + 1) * 256, :] = _dot_t(hidden, w2)
+    cell, owner, cap = listed_ref[:, 0, :], listed_ref[:, 1, :], listed_ref[:, 2, :]
+    named = owner == me_ref[0] * 32 + me_ref[1]
+    rank = _rank(named)
+    home = (cell % 32) // 8 + 1
     lane = lax.broadcasted_iota(jnp.int32, (32, 128), 1)
-    power = jnp.zeros((32, 128), F32)
-    sums = []
+    values = []
     for k in range(8):
         logit = logit_s[pl.ds(k, 128, stride=8), :]
-        cap = cap_ref[:, k : k + 1]
-        value = jnp.maximum(logit, 0.0) + jnp.log1p(jnp.exp(-jnp.abs(logit)))
-        value = jnp.where(cap > 0, value, 0.0)
-        weighted = value * (cap * 0.001)
-        fold = lambda a: (a[0:32] + a[32:64]) + (a[64:96] + a[96:128])
-        sums.append(fold(value))
-        power = power + fold(weighted)
-    total = jnp.sum(power, axis=0, keepdims=True)
+        values.append(jnp.maximum(logit, 0.0) + jnp.log1p(jnp.exp(-jnp.abs(logit))))
+    total = jnp.zeros((1, 128), F32)
+    found = []
+    for m in range(2):
+        one = named & (rank == m)
+        homes = jnp.sum(jnp.where(one, home, 0), axis=1, keepdims=True) - 1
+        caps = jnp.sum(jnp.where(one, cap, 0), axis=1, keepdims=True).astype(F32) * 0.001
+        for b in range(4):
+            value = jnp.zeros((32, 128), F32)
+            for d in range(4):
+                h = (b - d) % 4
+                value = jnp.where(
+                    homes[32 * b : 32 * b + 32] == h, values[2 * d + m][32 * h : 32 * h + 32], value
+                )
+            found.append(value)
+            total = total + jnp.sum(value * caps[32 * b : 32 * b + 32], axis=0, keepdims=True)
     for b in range(4):
-        rows = jnp.where(lane == 0, sums[2 * b], jnp.where(lane == 1, sums[2 * b + 1], total))
+        rows = jnp.where(lane == 0, found[b], jnp.where(lane == 1, found[4 + b], total))
         out_ref[32 * b : 32 * b + 32, :] = rows
 
 
-def decode(features, w1, w2, caps):
+def decode(features, w1, w2, listed, me):
     return pl.pallas_call(
         _decode_kernel,
         out_shape=jax.ShapeDtypeStruct((128, 128), F32),
+        in_specs=[VM] * 4 + [SM],
+        out_specs=VM,
         scratch_shapes=[pltpu.VMEM((1024, 128), F32)],
         compiler_params=pltpu.CompilerParams(vmem_limit_bytes=VMEM_LIMIT),
         cost_estimate=pl.CostEstimate(flops=600_000_000, bytes_accessed=2_000_000, transcendentals=600_000),
         name="decode",
-    )(features, w1, w2, caps)
-
-
-def _power_kernel(back_ref, owner_ref, slot_ref, cap_ref, power_ref, fleet_ref):
+    )(features, w1, w2, listed, me)
+
+
+def _power_kernel(back_ref, listed_ref, me_ref, power_ref, fleet_ref):
     back = back_ref[...]
-    named = lax.broadcasted_iota(jnp.int32, (128, 128), 0) == owner_ref[...]
-    first = jnp.sum(jnp.where(named, back[:, 0:1], 0.0), axis=0, keepdims=True)
-    second = jnp.sum(jnp.where(named, back[:, 1:2], 0.0), axis=0, keepdims=True)
-    value = jnp.where(slot_ref[...] == 0, first, second)
-    power_ref[...] = cap_ref[...].astype(F32) * 0.001 * value
-    fleet_ref[...] = jnp.sum(back, axis=0, keepdims=True) / 16384.0
-
-
-def power(back, owner, slot, cap):
+    mine = me_ref[0] * 32 + me_ref[1]
+    named = lax.broadcasted_iota(jnp.int32, (128, 128), 0) == listed_ref[mine, 1:2, :]
+    rank = _rank(named)
+    value = jnp.where(named, jnp.where(rank == 0, back[:, 0:1], back[:, 1:2]), 0.0)
+    kilowatts = listed_ref[mine, 2:3, :].astype(F32)
+    power_ref[...] = kilowatts * 0.001 * jnp.sum(value, axis=0, keepdims=True)
+    fleet_ref[...] = jnp.sum(back[:, 2:3], axis=0, keepdims=True) / 16384.0
+
+
+def power(back, listed, me):
     return pl.pallas_call(
         _power_kernel,
-        out_shape=(jax.ShapeDtypeStruct((1, 128), F32), jax.ShapeDtypeStruct((1, 128), F32)),
+        out_shape=(jax.ShapeDtypeStruct((1, 128), F32), jax.ShapeDtypeStruct((1, 1), F32)),
+        in_specs=[VM, VM, SM],
+        out_specs=(VM, VM),
         name="plant_power",
-    )(back, owner, slot, cap)
+    )(back, listed, me)
+
+
+def _assemble_kernel(p0_ref, p1_ref, p2_ref, p3_ref, me_ref, out_ref, sems):
+    copies = []
+    for d, p_ref in enumerate((p0_ref, p1_ref, p2_ref, p3_ref)):
+        place = lax.rem(me_ref[0] + 4 - d, 4)
+        copies.append(pltpu.make_async_copy(p_ref, out_ref.at[:, place], sems.at[d]))
+    for copy in copies:
+        copy.start()
+    for copy in copies:
+        copy.wait()
+
+
+def assemble(parts, me):
+    return pl.pallas_call(
+        _assemble_kernel,
+        out_shape=jax.ShapeDtypeStruct((64, 4, 8, 512), BF),
+        in_specs=[ANY] * 4 + [SM],
+        out_specs=ANY,
+        scratch_shapes=[pltpu.SemaphoreType.DMA((4,))],
+        name="assemble",
+    )(*parts, me)
 
 
 def body(
@@ -238,40 +294,24 @@
     seg = jnp.where(seg_of[:, None] == seg_of[None, :], 1.0 / 64, 0.0).astype(BF)
     tokens = a2a(cloud_field.reshape(32, 2, 32, 512), "strip")
 
-    owner = plant_decoder_device[:, 0]
-    listed = lax.all_gather(jnp.stack([plant_cell, owner, plant_capacity]), "band")
-    cell_all, owner_all, cap_all = listed[:, 0], listed[:, 1], listed[:, 2]
-    earlier = jnp.arange(128)[None, :] < jnp.arange(128)[:, None]
-    same = (owner_all[:, :, None] == owner_all[:, None, :]) & earlier[None]
-    slot_all = jnp.sum(same.astype(jnp.int32), axis=2)
-    mine = (cell_all % 32) // 8 == lax.axis_index("band")
-    token = jnp.where(mine, (cell_all // 32) * 8 + cell_all % 8, -1)
-    there = (owner_all[:, None, :] == jnp.arange(128)[None, :, None])[:, :, None, :] & (
-        slot_all[:, None, None, :] == jnp.arange(2)[None, None, :, None]
-    )
-    there = there & mine[:, None, None, :]
-    idx = jnp.sum(jnp.where(there, token[:, None, None, :] + 1, 0), axis=-1) - 1
-    caps = jnp.sum(jnp.where(there, cap_all[:, None, None, :], 0), axis=-1).astype(F32)
-    idx = idx.transpose(1, 0, 2).reshape(128, 8)
-    caps = caps.transpose(1, 0, 2).reshape(128, 8)
-    caps = jnp.pad(caps, ((0, 0), (0, 120))).reshape(128, 1, 128)
-    caps = a2a(caps, everyone).reshape(128, 128)
-    my_same = (owner[:, None] == owner[None, :]) & earlier.T
-    my_slot = jnp.sum(my_same.astype(jnp.int32), axis=0)
+    me = jnp.stack([lax.axis_index("band"), lax.axis_index("strip")]).astype(jnp.int32)
+    listed = jnp.stack([plant_cell, plant_decoder_device[:, 0], plant_capacity])
+    listed = lax.all_gather(jnp.pad(listed, ((0, 13), (0, 0))), everyone)
 
     row_args = (row_gain.reshape(1, 512), row_qkv, row_out, seg)
     sent0 = a2a(row_layer(tokens, 0, *row_args).reshape(128, 8, 512), everyone)
     sent1 = a2a(row_layer(tokens, 1, *row_args).reshape(128, 8, 512), everyone)
-    columns, features = col_layer(sent0, sent1, col_gain.reshape(1, 512), col_qkv, col_out, seg, idx)
+    *columns, features = col_layer(sent0, sent1, col_gain.reshape(1, 512), col_qkv, col_out, seg, listed, me)
     features = a2a(features, everyone)
-    field = a2a(columns.reshape(4, 64, 8, 512), "band")
-    final_field = field.transpose(1, 0, 2, 3).reshape(64, 32, 512)
-    payload = decode(features, decode_first, decode_second, caps)
+    columns = [c.reshape(64, 8, 512) for c in columns]
+    parts = columns[:1] + [
+        lax.ppermute(columns[d], "band", [(i, (i + d) % 4) for i in range(4)]) for d in (1, 2, 3)
+    ]
+    final_field = assemble(parts, me).reshape(64, 32, 512)
+    payload = decode(features, decode_first, decode_second, listed, me)
     back = a2a(payload.reshape(128, 1, 128), everyone).reshape(128, 128)
-    plant_power, fleet = power(
-        back, owner.reshape(1, 128), my_slot.reshape(1, 128), plant_capacity.reshape(1, 128)
-    )
-    return (final_field, plant_power.reshape(128), fleet[0, 2])
+    plant_power, fleet = power(back, listed, me)
+    return (final_field, plant_power.reshape(128), fleet.reshape(()))
 
 
 def solution(mesh):

time: 216 us -> 265 us (1.23); the launches traced: 214 us -> 260 us
  Pallas kernels: 61.5 us -> 132 us
  blocking collectives: 53.5 us -> 0 us
  between operations: 0.79 us -> 14.4 us
  starting transfers between devices: 30.5 us -> 40.1 us
  waiting for transfers between devices: 60 us -> 67.1 us
    pallas_call x1 -> x2, Pallas kernels: 24 us -> 85.3 us  [the longest x1 65.3 us: assemble(): pl.pallas_call(_assemble_kernel, out_shape=jax.ShapeDtypeStruct((64, 4, 8...]
    all_to_all x2 -> x0, blocking collectives: 44.4 us -> none  [body(): lax.all_to_all(x, axis, split_axis=0, concat_axis=0, tiled=True)]
    all_gather x1 -> x0, blocking collectives: 9.11 us -> none  [body(): lax.all_gather(jnp.stack([plant_cell, owner, plant_capacity]), 'band')]
    ppermute x0 -> x3, waiting for transfers between devices: none -> 7.71 us  [body(): lax.ppermute(columns[d], 'band', [(i, (i + d) % 4) for i in range(4)])]
    pallas_call x2, Pallas kernels: 32.5 us -> 39.7 us  [row_layer(): pl.pallas_call(_row_kernel, grid=(1,), out_shape=jax.ShapeDtypeStruct((4,...]
    ppermute x0 -> x3, starting transfers between devices: none -> 5.16 us  [body(): lax.ppermute(columns[d], 'band', [(i, (i + d) % 4) for i in range(4)])]
    all_to_all x5, starting transfers between devices: 30.5 us -> 34.9 us  [body(): lax.all_to_all(x, axis, split_axis=0, concat_axis=0, tiled=True)]
    unnamed x14 -> x24, local copies, waits for them, and re-layouts: 1.35 us -> 4.88 us
  transfers between devices with their start and end apart: 5 -> 9, of which waited for: 4 -> 4; matrix products, arithmetic and copies ran while one was open for 2% -> 1% of each run, Pallas kernels for 19% -> 42%
where the time goes in v1:
time: 265 us; the launch traced here: 260 us
  Pallas kernels  132 us (50%)
  waiting for transfers between devices  67.1 us (25%)
  starting transfers between devices  40.1 us (15%)
  between operations  14.4 us (5%)
  local copies, waits for them, and re-layouts  5.47 us (2%)
    pallas_call x1, Pallas kernels, assemble(): pl.pallas_call(_assemble_kernel, out_shape=jax.ShapeDtypeStruct((64, 4, 8...  65.3 us
    all_to_all x5, waiting for transfers between devices, body(): lax.all_to_all(x, axis, split_axis=0, concat_axis=0, tiled=True)  59.4 us
    pallas_call x2, Pallas kernels, row_layer(): pl.pallas_call(_row_kernel, grid=(1,), out_shape=jax.ShapeDtypeStruct((4,...  39.7 us
    all_to_all x5, starting transfers between devices, body(): lax.all_to_all(x, axis, split_axis=0, concat_axis=0, tiled=True)  34.9 us
    pallas_call x1, Pallas kernels, col_layer(): pl.pallas_call(_col_kernel, out_shape=(part,) * 4 + (jax.ShapeDtypeStruct...  20 us
    ppermute x3, waiting for transfers between devices, body(): lax.ppermute(columns[d], 'band', [(i, (i + d) % 4) for i in range(4)])  7.71 us
  transfers between devices with their start and end apart: 9, of which 4 were waited for; matrix products, arithmetic and copies ran while one was open for 1% of the time, Pallas kernels for 42%

profile of v1, /device:TPU:1, one launch (start us, length us, event | category | flops | bytes accessed | tf_op | source)
XLA Modules:
  0.0 260.3 jit_solution(5411394896126441192)
XLA Ops:
  7.2 0.0 copy-start.8
  7.2 0.0 copy-start.9
  7.2 0.0 copy-start.10
  7.2 9.6 %all-to-all-start = ((bf16[32,2,32,512]{3,2,1,0:T(8,128)(2,1)}), bf16[32,2,32,512]{3,2,1,0:T(8,128)(2,1)S(1)}, u32[]{:S(2)}, u32[]{:S(2)}) async-start(bf16[32,2,32,512]{3,2,1,0:T(8,128)(2,1)} %bitcast.25), calls=%async_computation | async-start | bytes 4194304 | tf_op jit(solution)/shard_map/all_to_all | solution.py:292
  16.8 0.0 all-gather.3.cloned.1.call-start
  16.8 0.0 copy-done.8
  16.8 0.0 copy-done.9
  16.8 0.0 copy-done.10
  16.9 0.6 pad.4
  17.5 0.0 all-gather.3.cloned.1.call-update
  17.5 0.8 select_convert_fusion.seg_ref
  18.3 26.8 %all-to-all-done.x_ref = bf16[32,2,32,512]{3,2,1,0:T(8,128)(2,1)S(1)} async-done(((bf16[32,2,32,512]{3,2,1,0:T(8,128)(2,1)}), bf16[32,2,32,512]{3,2,1,0:T(8,128)(2,1)S(1)}, u32[]{:S(2)}, u32[]{:S(2)}) %all-to-all-start) | async-done | bytes 2097184 | tf_op jit(solution)/shard_map/all_to_all | solution.py:292
  45.1 0.0 copy-start.1
  45.1 1.3 copy-done.1
  46.4 15.3 %row_layer.3 = bf16[4,32,8,512]{3,2,1,0:T(8,128)(2,1)} custom-call(bf16[32,2,32,512]{3,2,1,0:T(8,128)(2,1)} %copy-done.1, f32[1,512]{1,0:T(1,128)} %bitcast.36, bf16[512,1536]{1,0:T(8,128)(2,1)} %wqkv_ref.4, bf16[512,512]{1,0:T(8,128)(2,1)} %wo_ref.4, bf16[256,256]{1,0:T(8,128)(2,1)} %select_convert_fusion.seg_ref), custom_call_target="tpu_custom_call" | custom-call | flops 12000000000 | bytes 4000000 | tf_op jit(solution)/shard_map/row_layer/pallas_call | solution.py:101
  61.7 6.0 %all-to-all-start.2 = ((bf16[128,8,512]{2,1,0:T(8,128)(2,1)}), bf16[128,8,512]{2,1,0:T(8,128)(2,1)S(1)}, u32[]{:S(2)}, u32[]{:S(2)}) async-start(bf16[128,8,512]{2,1,0:T(8,128)(2,1)} %bitcast.28), calls=%async_computation.2 | async-start | bytes 2097152 | tf_op jit(solution)/shard_map/all_to_all | solution.py:292
  67.7 24.4 %row_layer.2 = bf16[4,32,8,512]{3,2,1,0:T(8,128)(2,1)} custom-call(bf16[32,2,32,512]{3,2,1,0:T(8,128)(2,1)} %copy-done.1, f32[1,512]{1,0:T(1,128)} %bitcast.37, bf16[512,1536]{1,0:T(8,128)(2,1)} %wqkv_ref.4, bf16[512,512]{1,0:T(8,128)(2,1)} %wo_ref.4, bf16[256,256]{1,0:T(8,128)(2,1)} %select_convert_fusion.seg_ref), custom_call_target="tpu_custom_call" | custom-call | flops 12000000000 | bytes 4000000 | tf_op jit(solution)/shard_map/row_layer/pallas_call | solution.py:101
  92.1 0.0 all-to-all-done.2.x1_ref
  92.1 0.0 copy-start.2
  92.1 9.8 %all-to-all-start.1 = ((bf16[128,8,512]{2,1,0:T(8,128)(2,1)}), bf16[128,8,512]{2,1,0:T(8,128)(2,1)S(1)}, u32[]{:S(2)}, u32[]{:S(2)}) async-start(bf16[128,8,512]{2,1,0:T(8,128)(2,1)} %bitcast.27), calls=%async_computation.1 | async-start | bytes 2097152 | tf_op jit(solution)/shard_map/all_to_all | solution.py:292
  101.9 0.7 pad_add_fusion.1.me_ref
  102.5 0.0 all-gather.3.cloned.1.call-done
  102.5 18.5 %all-to-all-done.1.x0_ref = bf16[128,8,512]{2,1,0:T(8,128)(2,1)S(1)} async-done(((bf16[128,8,512]{2,1,0:T(8,128)(2,1)}), bf16[128,8,512]{2,1,0:T(8,128)(2,1)S(1)}, u32[]{:S(2)}, u32[]{:S(2)}) %all-to-all-start.1) | async-done | bytes 1048608 | tf_op jit(solution)/shard_map/all_to_all | solution.py:292
  121.0 0.0 copy-start.3
  121.0 0.0 copy-done.2
  121.0 1.0 copy-done.3
  122.0 20.0 %col_layer.1 = (bf16[32,2,8,512]{3,2,1,0:T(8,128)(2,1)}, bf16[32,2,8,512]{3,2,1,0:T(8,128)(2,1)}, bf16[32,2,8,512]{3,2,1,0:T(8,128)(2,1)}, bf16[32,2,8,512]{3,2,1,0:T(8,128)(2,1)}, bf16[128,8,512]{2,1,0:T(8,128)(2,1)}) custom-call(bf16[128,8,512]{2,1,0:T(8,128)(2,1)} %copy-done.3, bf16[128,8,512]{2,1,0:T(8,128)(2,1)} %copy-done.2, f32[1,512]{1,0:T(1,128)} %bitcast.38, ...), custom_call_target="tpu_custom_call" | custom-call | flops 12000000000 | bytes 9000000 | tf_op jit(solution)/shard_map/col_layer/pallas_call | solution.py:184
  142.0 5.1 %all-to-all-start.3 = ((bf16[128,8,512]{2,1,0:T(8,128)(2,1)}), bf16[128,8,512]{2,1,0:T(8,128)(2,1)S(1)}, u32[]{:S(2)}, u32[]{:S(2)}) async-start(bf16[128,8,512]{2,1,0:T(8,128)(2,1)} %get-tuple-element.14), calls=%async_computation.3 | async-start | bytes 2097152 | tf_op jit(solution)/shard_map/all_to_all | solution.py:292
  147.1 1.5 collective-permute-start
  148.6 2.5 collective-permute-start.1
  151.1 0.0 copy-done.11
  151.1 1.1 collective-permute-start.2
  152.2 14.1 %all-to-all-done.3.f_ref = bf16[128,8,512]{2,1,0:T(8,128)(2,1)S(1)} async-done(((bf16[128,8,512]{2,1,0:T(8,128)(2,1)}), bf16[128,8,512]{2,1,0:T(8,128)(2,1)S(1)}, u32[]{:S(2)}, u32[]{:S(2)}) %all-to-all-start.3) | async-done | bytes 1048608 | tf_op jit(solution)/shard_map/all_to_all | solution.py:292
  166.3 1.0 copy-done
  167.3 4.8 %decode.1 = f32[128,128]{1,0:T(8,128)} custom-call(bf16[128,8,512]{2,1,0:T(8,128)(2,1)} %copy-done, bf16[512,512]{1,0:T(8,128)(2,1)} %w1_ref.1, bf16[1,512]{1,0:T(2,128)(2,1)} %w2_ref.1, s32[128,16,128]{2,1,0:T(8,128)} %bitcast.23, s32[2]{0:T(128)} %pad_add_fusion.1.me_ref), custom_call_target="tpu_custom_call" | custom-call | flops 600000000 | bytes 2000000 | tf_op jit(solution)/shard_map/decode/pallas_call | solution.py:232
  172.0 4.6 %all-to-all-start.4 = ((f32[128,1,128]{2,1,0:T(1,128)}), f32[128,1,128]{2,1,0:T(1,128)S(1)}, u32[]{:S(2)}, u32[]{:S(2)}) async-start(f32[128,1,128]{2,1,0:T(1,128)} %bitcast.31), calls=%async_computation.4 | async-start | bytes 131072 | tf_op jit(solution)/shard_map/all_to_all | solution.py:292
  176.6 0.0 collective-permute-done.p1_ref
  176.6 0.0 copy-start.4
  176.6 7.7 %collective-permute-done.1.p2_ref = bf16[64,8,512]{2,1,0:T(8,128)(2,1)S(1)} collective-permute-done((bf16[64,8,512]{2,1,0:T(8,128)(2,1)}, bf16[64,8,512]{2,1,0:T(8,128)(2,1)S(1)}, u32[]{:S(2)}, u32[]{:S(2)}) %collective-permute-start.1) | collective-permute-done | bytes 524320 | tf_op jit(solution)/shard_map/ppermute | solution.py:308
  184.4 0.0 collective-permute-done.2.p3_ref
  184.4 0.0 copy-done.4
  184.4 0.8 copy-done.5
  185.1 0.2 copy-done.6
  185.3 65.3 %assemble.1 = bf16[64,4,8,512]{3,2,1,0:T(8,128)(2,1)} custom-call(bf16[64,8,512]{2,1,0:T(8,128)(2,1)} %bitcast.29, bf16[64,8,512]{2,1,0:T(8,128)(2,1)} %copy-done.4, bf16[64,8,512]{2,1,0:T(8,128)(2,1)} %copy-done.5, bf16[64,8,512]{2,1,0:T(8,128)(2,1)} %copy-done.6, s32[2]{0:T(128)} %pad_add_fusion.1.me_ref), custom_call_target="tpu_custom_call" | custom-call | tf_op jit(solution)/shard_map/assemble/pallas_call | solution.py:277
  250.7 0.0 all-to-all-done.4
  250.7 0.0 copy-start.7
  250.7 0.6 copy-done.7
  251.3 1.9 plant_power.1
  (6 shorter events, 0.0 us)
Async XLA Ops:
  7.2 9.7 %copy-start.8 = (s32[128]{0:T(128)S(1)}, s32[128]{0:T(128)}, u32[]{:S(2)}) copy-start(s32[128]{0:T(128)} %param.21) | copy-start | bytes 1540
  7.2 9.7 %copy-start.9 = (s32[128,1]{0,1:T(1,128)S(1)}, s32[128,1]{0,1:T(1,128)}, u32[]{:S(2)}) copy-start(s32[128,1]{0,1:T(1,128)} %param.20) | copy-start | bytes 1540
  7.2 9.7 %copy-start.10 = (s32[128]{0:T(128)S(1)}, s32[128]{0:T(128)}, u32[]{:S(2)}) copy-start(s32[128]{0:T(128)} %param.19) | copy-start | bytes 1540
  7.2 37.9 %all-to-all-start = ((bf16[32,2,32,512]{3,2,1,0:T(8,128)(2,1)}), bf16[32,2,32,512]{3,2,1,0:T(8,128)(2,1)S(1)}, u32[]{:S(2)}, u32[]{:S(2)}) async-start(bf16[32,2,32,512]{3,2,1,0:T(8,128)(2,1)} %bitcast.25), calls=%async_computation | async-start | bytes 4194304 | tf_op jit(solution)/shard_map/all_to_all | solution.py:292
  16.8 85.8 %all-gather.3.cloned.1.call-start = ((), (), s32[]{:S(2)}) async-start(), calls=%async_computation.5 | async-start | bytes 1056768 | tf_op jit(solution)/shard_map/all_gather | solution.py:299
  45.1 1.3 copy-start.1
  61.7 30.4 %all-to-all-start.2 = ((bf16[128,8,512]{2,1,0:T(8,128)(2,1)}), bf16[128,8,512]{2,1,0:T(8,128)(2,1)S(1)}, u32[]{:S(2)}, u32[]{:S(2)}) async-start(bf16[128,8,512]{2,1,0:T(8,128)(2,1)} %bitcast.28), calls=%async_computation.2 | async-start | bytes 2097152 | tf_op jit(solution)/shard_map/all_to_all | solution.py:292
  92.1 28.9 %copy-start.2 = (bf16[128,8,512]{2,1,0:T(8,128)(2,1)}, bf16[128,8,512]{2,1,0:T(8,128)(2,1)S(1)}, u32[]{:S(2)}) copy-start(bf16[128,8,512]{2,1,0:T(8,128)(2,1)S(1)} %all-to-all-done.2.x1_ref) | copy-start | bytes 3145732
  92.1 28.9 %all-to-all-start.1 = ((bf16[128,8,512]{2,1,0:T(8,128)(2,1)}), bf16[128,8,512]{2,1,0:T(8,128)(2,1)S(1)}, u32[]{:S(2)}, u32[]{:S(2)}) async-start(bf16[128,8,512]{2,1,0:T(8,128)(2,1)} %bitcast.27), calls=%async_computation.1 | async-start | bytes 2097152 | tf_op jit(solution)/shard_map/all_to_all | solution.py:292
  121.0 1.0 copy-start.3
  142.0 9.1 %copy-start.11 = (bf16[32,2,8,512]{3,2,1,0:T(8,128)(2,1)S(1)}, bf16[32,2,8,512]{3,2,1,0:T(8,128)(2,1)}, u32[]{:S(2)}) copy-start(bf16[32,2,8,512]{3,2,1,0:T(8,128)(2,1)} %get-tuple-element.13) | copy-start | bytes 1572868
  142.0 24.3 %all-to-all-start.3 = ((bf16[128,8,512]{2,1,0:T(8,128)(2,1)}), bf16[128,8,512]{2,1,0:T(8,128)(2,1)S(1)}, u32[]{:S(2)}, u32[]{:S(2)}) async-start(bf16[128,8,512]{2,1,0:T(8,128)(2,1)} %get-tuple-element.14), calls=%async_computation.3 | async-start | bytes 2097152 | tf_op jit(solution)/shard_map/all_to_all | solution.py:292
  147.1 29.5 %collective-permute-start = (bf16[64,8,512]{2,1,0:T(8,128)(2,1)}, bf16[64,8,512]{2,1,0:T(8,128)(2,1)S(1)}, u32[]{:S(2)}, u32[]{:S(2)}) collective-permute-start(bf16[64,8,512]{2,1,0:T(8,128)(2,1)} %bitcast.12), channel_id=1, source_target_pairs={{0,32},{32,64},{64,96},{96,0},{1,33},{33,65},{65,97},{97,1},{2,34}... | collective-permute-start | bytes 1572872 | tf_op jit(solution)/shard_map/ppermute | solution.py:308
  148.6 35.8 %collective-permute-start.1 = (bf16[64,8,512]{2,1,0:T(8,128)(2,1)}, bf16[64,8,512]{2,1,0:T(8,128)(2,1)S(1)}, u32[]{:S(2)}, u32[]{:S(2)}) collective-permute-start(bf16[64,8,512]{2,1,0:T(8,128)(2,1)} %bitcast.13), channel_id=1, source_target_pairs={{0,64},{32,96},{64,0},{96,32},{1,65},{33,97},{65,1},{97,33},{2,66}... | collective-permute-start | bytes 1572872 | tf_op jit(solution)/shard_map/ppermute | solution.py:308
  151.1 33.2 %collective-permute-start.2 = (bf16[64,8,512]{2,1,0:T(8,128)(2,1)S(1)}, bf16[64,8,512]{2,1,0:T(8,128)(2,1)S(1)}, u32[]{:S(2)}, u32[]{:S(2)}) collective-permute-start(bf16[64,8,512]{2,1,0:T(8,128)(2,1)S(1)} %bitcast.35), channel_id=1, source_target_pairs={{0,96},{32,0},{64,32},{96,64},{1,97},{33,1},{65,33},{97,65},{2,98}... | collective-permute-start | bytes 1572872 | tf_op jit(solution)/shard_map/ppermute | solution.py:308
  166.3 1.0 copy-start
  172.0 78.6 %all-to-all-start.4 = ((f32[128,1,128]{2,1,0:T(1,128)}), f32[128,1,128]{2,1,0:T(1,128)S(1)}, u32[]{:S(2)}, u32[]{:S(2)}) async-start(f32[128,1,128]{2,1,0:T(1,128)} %bitcast.31), calls=%async_computation.4 | async-start | bytes 131072 | tf_op jit(solution)/shard_map/all_to_all | solution.py:292
  176.6 7.7 %copy-start.4 = (bf16[64,8,512]{2,1,0:T(8,128)(2,1)}, bf16[64,8,512]{2,1,0:T(8,128)(2,1)S(1)}, u32[]{:S(2)}) copy-start(bf16[64,8,512]{2,1,0:T(8,128)(2,1)S(1)} %collective-permute-done.p1_ref) | copy-start | bytes 1572868
  184.3 0.8 copy-start.5
  184.4 1.0 copy-start.6
  250.7 0.6 copy-start.7
Sparse Core Ops, SparseCore 0:
  20.4 73.5 all-gather.2
